TPU v7x, 32 devices: a whole 2x2x4 slice. The times are simulated.
32 devices in a mesh: rep: 8 (over z, core), shard: 4 (over y, x).
Axes of the slice: x: 2, y: 2, z: 4, core: 2. Of those that a mesh axis runs over, the one named last changes fastest.
Arguments:
- tokens: bfloat16 [4096, 1024], P(('rep', 'shard')), may hold values from -6 to 6
- cotangent: bfloat16 [4096, 1024], P(('rep', 'shard')), may hold values from -6 to 6
- seq_len: int32 [128], P(('rep', 'shard')), may hold values from 0 to 128, as said below
- in_proj: float32 [1024, 4096], P('shard'), may hold values from -0.1875 to 0.1875
- in_proj_first: float32 [1024, 4096], P('shard', 'rep'), may hold values from -0.0390625 to 0.0390625
- in_proj_second: float32 [1024, 4096], P('shard', 'rep'), may hold values from 1.2207031e-05 to 0.00021972656
- dt_proj: float32 [1024, 24], P('shard'), may hold values from -0.1875 to 0.1875
- dt_proj_first: float32 [1024, 24], P('shard'), may hold values from -0.0390625 to 0.0390625
- dt_proj_second: float32 [1024, 24], P('shard'), may hold values from 1.2207031e-05 to 0.00021972656
- out_proj: float32 [2048, 1024], P('shard'), may hold values from -0.125 to 0.125
- out_proj_first: float32 [2048, 1024], P('shard', 'rep'), may hold values from -0.0390625 to 0.0390625
- out_proj_second: float32 [2048, 1024], P('shard', 'rep'), may hold values from 1.2207031e-05 to 0.00021972656
- gate_up: float32 [1024, 4096], P('shard'), may hold values from -0.1875 to 0.1875
- gate_up_first: float32 [1024, 4096], P('shard', 'rep'), may hold values from -0.0390625 to 0.0390625
- gate_up_second: float32 [1024, 4096], P('shard', 'rep'), may hold values from 1.2207031e-05 to 0.00021972656
- down_proj: float32 [2048, 1024], P('shard'), may hold values from -0.125 to 0.125
- down_proj_first: float32 [2048, 1024], P('shard', 'rep'), may hold values from -0.0390625 to 0.0390625
- down_proj_second: float32 [2048, 1024], P('shard', 'rep'), may hold values from 1.2207031e-05 to 0.00021972656
- norm_gains: float32 [3584], P('shard'), may hold values from 0.5 to 1.5
- gains_first: float32 [3584], P('shard'), may hold values from -0.0390625 to 0.0390625
- gains_second: float32 [3584], P('shard'), may hold values from 1.2207031e-05 to 0.00021972656
- conv_taps: float32 [5, 1792], P(None, 'shard'), may hold values from -3 to 3
- conv_first: float32 [5, 1792], P(None, 'shard'), may hold values from -0.0390625 to 0.0390625
- conv_second: float32 [5, 1792], P(None, 'shard'), may hold values from 1.2207031e-05 to 0.00021972656
- ssm_params: float32 [3, 24], replicated, may hold values from -4.5 to 3, as said below
- ssm_first: float32 [3, 24], replicated, may hold values from -0.3125 to 0.3125
- ssm_second: float32 [3, 24], replicated, may hold values from 0.00012207031 to 0.0009765625
Outputs:
- output: bfloat16 [4096, 1024], P(('rep', 'shard'))
- token_grad: bfloat16 [4096, 1024], P(('rep', 'shard'))
- in_proj_first_new: float32 [1024, 4096], P('shard', 'rep')
- in_proj_second_new: float32 [1024, 4096], P('shard', 'rep')
- in_proj_new: float32 [1024, 4096], P('shard')
- dt_proj_first_new: float32 [1024, 24], P('shard')
- dt_proj_second_new: float32 [1024, 24], P('shard')
- dt_proj_new: float32 [1024, 24], P('shard')
- out_proj_first_new: float32 [2048, 1024], P('shard', 'rep')
- out_proj_second_new: float32 [2048, 1024], P('shard', 'rep')
- out_proj_new: float32 [2048, 1024], P('shard')
- gate_up_first_new: float32 [1024, 4096], P('shard', 'rep')
- gate_up_second_new: float32 [1024, 4096], P('shard', 'rep')
- gate_up_new: float32 [1024, 4096], P('shard')
- down_proj_first_new: float32 [2048, 1024], P('shard', 'rep')
- down_proj_second_new: float32 [2048, 1024], P('shard', 'rep')
- down_proj_new: float32 [2048, 1024], P('shard')
- gains_first_new: float32 [3584], P('shard')
- gains_second_new: float32 [3584], P('shard')
- gains_new: float32 [3584], P('shard')
- conv_first_new: float32 [5, 1792], P(None, 'shard')
- conv_second_new: float32 [5, 1792], P(None, 'shard')
- conv_new: float32 [5, 1792], P(None, 'shard')
- ssm_first_new: float32 [3, 24], replicated
- ssm_second_new: float32 [3, 24], replicated
- ssm_new: float32 [3, 24], replicated
Inputs may be any that keep to these rules, and one draw needn't show every extreme that they name: `seq_len`: each device's 4 lengths sum to at most 128; the last device holds one sequence of exactly 128 tokens and its other slots are empty. `ssm_params`: row 0 holds log decay rates, row 1 step offsets, row 2 skip gains.
All inputs are finite; a program needn't handle non-finite values.
Results may differ from a plain program's by a relative error of at most 0.011.
The roundings to bfloat16 on the way count: a program that leaves them out, or rounds other values in their place, can miss the bound.
Values may be sent and summed in bfloat16 or wider, within the bound.
A program may use at most 128 MiB of HBM per device.

v0:
```python
import jax
import jax.numpy as jnp
from jax import lax
from jax.sharding import PartitionSpec as P

D = 1024
MIXER_HEADS = 24
MIXER_HEAD_SIZE = 64
NS = 128
QUERY_HEADS = 8
KEY_VALUE_HEADS = 2
HEAD_SIZE = 64
FF = 2048
KCONV = 4
STEP = 10
MIXER_WIDTH = 1536
CONV = 1792
NOUT = 2048


precise = lax.Precision.HIGHEST
EPSILON_NORM = 1e-05
ROPE_BASE = 10000.0
NEG_BIG = -1e30
ATT_MULT = 8.0
BETA_ONE = 0.9
BETA_TWO = 0.95
ADAM_EPS = 1e-08


def rms_scale(values, gain):
    return (
        values * lax.rsqrt(jnp.mean(values * values, axis=-1, keepdims=True) + EPSILON_NORM) * gain
    )


def layout(lengths, count_of_rows):
    seq_ends = jnp.cumsum(lengths)
    starts = seq_ends - lengths
    row_ids = jnp.arange(count_of_rows, dtype=jnp.int32)
    document = jnp.sum((row_ids[:, None] >= seq_ends[None, :]).astype(jnp.int32), axis=1)
    row_alive = row_ids < seq_ends[-1]
    slot_ids = jnp.arange(lengths.shape[0], dtype=jnp.int32)
    first_row = jnp.sum(
        jnp.where(document[:, None] == slot_ids[None, :], starts[None, :], 0), axis=1
    )
    token_position = jnp.where(row_alive, row_ids - first_row, 0)
    same_doc = (
        (document[:, None] == document[None, :])
        & row_alive[None, :]
        & (row_ids[None, :] <= row_ids[:, None])
    )
    pair_mask = same_doc | (row_ids[:, None] == row_ids[None, :])
    return (row_alive, token_position, pair_mask)


def apply_rotary(head_rows, token_position):
    half_width = head_rows.shape[-1] // 2
    frequency = ROPE_BASE ** (-jnp.arange(half_width, dtype=jnp.float32) / half_width)
    angles = token_position.astype(jnp.float32)[:, None] * frequency[None, :]
    cosine = jnp.cos(angles)[:, None, :]
    sine_part = jnp.sin(angles)[:, None, :]
    front = head_rows[..., :half_width]
    latter = head_rows[..., half_width:]
    return jnp.concatenate(
        [front * cosine - latter * sine_part, latter * cosine + front * sine_part], axis=-1
    )


def rotary_pair(query_key_pair, token_position):
    count_of_rows = query_key_pair.shape[0]
    head_rows = query_key_pair.reshape(count_of_rows, QUERY_HEADS + KEY_VALUE_HEADS, HEAD_SIZE)
    return apply_rotary(head_rows, token_position).reshape(
        count_of_rows, (QUERY_HEADS + KEY_VALUE_HEADS) * HEAD_SIZE
    )


def swiglu(gate_vals):
    return jax.nn.silu(gate_vals[:, :FF]) * gate_vals[:, FF:]


def mixer_core(zxbc, conv_weight, ssm_weight, gain_mix, pair_mask, token_position):
    count_of_rows = zxbc.shape[0]
    gate_z = zxbc[:, :MIXER_WIDTH]
    conv_in = zxbc[:, MIXER_WIDTH : MIXER_WIDTH + CONV]
    dt_raw = zxbc[:, MIXER_WIDTH + CONV : MIXER_WIDTH + CONV + MIXER_HEADS]
    conv_sum = jnp.broadcast_to(conv_weight[KCONV][None, :], conv_in.shape)
    for tap_index in range(KCONV):
        lag_rows = KCONV - 1 - tap_index
        if lag_rows == 0:
            shifted = conv_in
        else:
            shifted = jnp.concatenate(
                [jnp.zeros((lag_rows, CONV), conv_in.dtype), conv_in[: count_of_rows - lag_rows]],
                axis=0,
            )
            shifted = jnp.where((token_position >= lag_rows)[:, None], shifted, 0.0)
        conv_sum = conv_sum + conv_weight[tap_index][None, :] * shifted
    convolved_output = jax.nn.silu(conv_sum)
    input_heads = convolved_output[:, :MIXER_WIDTH].reshape(
        count_of_rows, MIXER_HEADS, MIXER_HEAD_SIZE
    )
    b_rows = convolved_output[:, MIXER_WIDTH : MIXER_WIDTH + NS]
    c_rows = convolved_output[:, MIXER_WIDTH + NS :]
    dt_step = jax.nn.softplus(dt_raw + ssm_weight[1][None, :])
    decay_rate = -jnp.exp(ssm_weight[0])
    decay_cum = jnp.cumsum(dt_step * decay_rate[None, :], axis=0).T
    decay_gaps = decay_cum[:, :, None] - decay_cum[:, None, :]
    weights = jnp.exp(jnp.where(pair_mask[None], decay_gaps, NEG_BIG))
    inner_prod = jnp.dot(c_rows, b_rows.T, precision=precise)
    kernel = weights * inner_prod[None] * dt_step.T[:, None, :]
    mixed_out = jnp.einsum("hts,shd->thd", kernel, input_heads, precision=precise)
    mixed_out = mixed_out + ssm_weight[2][None, :, None] * input_heads
    gated_out = mixed_out.reshape(count_of_rows, MIXER_WIDTH) * jax.nn.silu(gate_z)
    return rms_scale(gated_out, gain_mix)


def masked_scores(query_rows, key_reduced, pair_mask):
    scores = jnp.einsum(
        "tkgd,skd->kgts", query_rows, key_reduced, preferred_element_type=jnp.float32
    ) * HEAD_SIZE ** (-0.5)
    return jnp.where(pair_mask[None, None], scores, NEG_BIG)


def left_product(left, right):
    return lax.dot_general(
        left, right, (((0,), (0,)), ((), ())), preferred_element_type=jnp.float32
    )


def right_product(left, right):
    return lax.dot_general(
        left, right, (((1,), (1,)), ((), ())), preferred_element_type=jnp.float32
    )


def adam_update(param, first, second, grad, rate, decay):
    new_first = BETA_ONE * first + (1.0 - BETA_ONE) * grad
    new_second = BETA_TWO * second + (1.0 - BETA_TWO) * grad * grad
    first_hat = new_first / (1.0 - BETA_ONE**STEP)
    second_hat = new_second / (1.0 - BETA_TWO**STEP)
    new_param = param - rate * (first_hat / (jnp.sqrt(second_hat) + ADAM_EPS) + decay * param)
    return (new_first, new_second, new_param)


def column_block(whole_rows, like, block_index):
    width = like.shape[1]
    return lax.dynamic_slice_in_dim(whole_rows, block_index * width, width, 1)


def local(
    tokens,
    cotangent,
    seq_len,
    in_proj,
    in_proj_first,
    in_proj_second,
    dt_proj,
    dt_proj_first,
    dt_proj_second,
    out_proj,
    out_proj_first,
    out_proj_second,
    gate_up,
    gate_up_first,
    gate_up_second,
    down_proj,
    down_proj_first,
    down_proj_second,
    norm_gains,
    gains_first,
    gains_second,
    conv_taps,
    conv_first,
    conv_second,
    ssm_params,
    ssm_first,
    ssm_second,
):
    token_local = jnp.sum(seq_len).astype(jnp.float32)
    token_count = lax.psum(token_local, ("rep", "shard"))
    full_in, full_dt, full_out, full_gu, full_down, full_gains, full_conv = (
        lax.all_gather(in_proj.astype(jnp.bfloat16), "shard", axis=0, tiled=True),
        lax.all_gather(dt_proj.astype(jnp.bfloat16), "shard", axis=0, tiled=True),
        lax.all_gather(out_proj.astype(jnp.bfloat16), "shard", axis=0, tiled=True),
        lax.all_gather(gate_up.astype(jnp.bfloat16), "shard", axis=0, tiled=True),
        lax.all_gather(down_proj.astype(jnp.bfloat16), "shard", axis=0, tiled=True),
        lax.all_gather(norm_gains.astype(jnp.bfloat16), "shard", axis=0, tiled=True),
        lax.all_gather(conv_taps.astype(jnp.bfloat16), "shard", axis=1, tiled=True),
    )
    count_of_rows = tokens.shape[0]
    row_alive, token_position, pair_mask = layout(seq_len, count_of_rows)
    inputs = tokens.astype(jnp.float32)
    gains_full = full_gains.astype(jnp.float32)
    conv_full = full_conv.astype(jnp.float32)
    normed_value, norm_back = jax.vjp(rms_scale, inputs, gains_full[:D])
    normed = normed_value.astype(jnp.bfloat16)
    main_proj = jnp.dot(normed, full_in, preferred_element_type=jnp.float32)
    dt_raw = jnp.dot(normed, full_dt, preferred_element_type=jnp.float32)
    projected_input = jnp.concatenate(
        [main_proj[:, : MIXER_WIDTH + CONV], dt_raw, main_proj[:, MIXER_WIDTH + CONV :]], axis=1
    )
    split_boundary = MIXER_WIDTH + CONV + MIXER_HEADS
    mixer_value, mixer_back = jax.vjp(
        lambda proj_part, conv_part, ssm_part, gain_part: mixer_core(
            proj_part, conv_part, ssm_part, gain_part, pair_mask, token_position
        ),
        projected_input[:, :split_boundary],
        conv_full,
        ssm_params,
        gains_full[2 * D :],
    )
    mixer_low = mixer_value.astype(jnp.bfloat16)
    rotary_output, rope_back = jax.vjp(
        lambda query_key_pair: rotary_pair(query_key_pair, token_position),
        projected_input[
            :, split_boundary : split_boundary + (QUERY_HEADS + KEY_VALUE_HEADS) * HEAD_SIZE
        ],
    )
    query_group_width = QUERY_HEADS // KEY_VALUE_HEADS
    query_rows = (
        rotary_output[:, : QUERY_HEADS * HEAD_SIZE]
        .astype(jnp.bfloat16)
        .reshape(count_of_rows, KEY_VALUE_HEADS, query_group_width, HEAD_SIZE)
    )
    key_reduced = (
        rotary_output[:, QUERY_HEADS * HEAD_SIZE :]
        .astype(jnp.bfloat16)
        .reshape(count_of_rows, KEY_VALUE_HEADS, HEAD_SIZE)
    )
    value_reduced = (
        projected_input[:, split_boundary + (QUERY_HEADS + KEY_VALUE_HEADS) * HEAD_SIZE :]
        .astype(jnp.bfloat16)
        .reshape(count_of_rows, KEY_VALUE_HEADS, HEAD_SIZE)
    )
    scores = masked_scores(query_rows, key_reduced, pair_mask)
    log_total = jax.nn.logsumexp(scores, axis=-1, keepdims=True)
    probs_low = jnp.exp(scores - log_total).astype(jnp.bfloat16)
    attended = jnp.einsum(
        "kgts,skd->tkgd", probs_low, value_reduced, preferred_element_type=jnp.float32
    )
    attended_low = attended.reshape(count_of_rows, QUERY_HEADS * HEAD_SIZE).astype(jnp.bfloat16)
    branch_in = jnp.concatenate([mixer_low, attended_low * ATT_MULT], axis=1)
    branch = jnp.dot(branch_in, full_out, preferred_element_type=jnp.float32)
    hidden = inputs + branch
    normed_two_value, norm_two_back = jax.vjp(rms_scale, hidden, gains_full[D : 2 * D])
    normed_two = normed_two_value.astype(jnp.bfloat16)
    gate_vals = jnp.dot(normed_two, full_gu, preferred_element_type=jnp.float32)
    act_value, swiglu_back = jax.vjp(swiglu, gate_vals)
    act_low = act_value.astype(jnp.bfloat16)
    output = hidden + jnp.dot(act_low, full_down, preferred_element_type=jnp.float32)
    back_in, back_dt, back_out, back_gu, back_down = (
        lax.all_gather(in_proj.astype(jnp.bfloat16), "shard", axis=0, tiled=True),
        lax.all_gather(dt_proj.astype(jnp.bfloat16), "shard", axis=0, tiled=True),
        lax.all_gather(out_proj.astype(jnp.bfloat16), "shard", axis=0, tiled=True),
        lax.all_gather(gate_up.astype(jnp.bfloat16), "shard", axis=0, tiled=True),
        lax.all_gather(down_proj.astype(jnp.bfloat16), "shard", axis=0, tiled=True),
    )
    upstream = cotangent.astype(jnp.float32) * row_alive[:, None].astype(jnp.float32)
    upstream_low = upstream.astype(jnp.bfloat16)
    grad_down = left_product(act_low, upstream_low)
    d_act = right_product(upstream_low, back_down)
    (d_gate_vals,) = swiglu_back(d_act)
    d_gate_low = d_gate_vals.astype(jnp.bfloat16)
    grad_gu = left_product(normed_two, d_gate_low)
    d_normed_two = right_product(d_gate_low, back_gu)
    d_hidden_norm, d_gain_two = norm_two_back(d_normed_two)
    d_hidden = upstream + d_hidden_norm
    d_branch_low = d_hidden.astype(jnp.bfloat16)
    grad_out = left_product(branch_in, d_branch_low)
    d_branch_in = right_product(d_branch_low, back_out)
    mixer_projection_gradient, d_conv, d_ssm, d_gain_mix = mixer_back(d_branch_in[:, :MIXER_WIDTH])
    d_attended = (
        (d_branch_in[:, MIXER_WIDTH:] * ATT_MULT)
        .astype(jnp.bfloat16)
        .reshape(count_of_rows, KEY_VALUE_HEADS, query_group_width, HEAD_SIZE)
    )
    probs = jnp.exp(masked_scores(query_rows, key_reduced, pair_mask) - log_total)
    d_probs = jnp.einsum(
        "tkgd,skd->kgts", d_attended, value_reduced, preferred_element_type=jnp.float32
    )
    value_gradient = jnp.einsum(
        "kgts,tkgd->skd", probs.astype(jnp.bfloat16), d_attended, preferred_element_type=jnp.float32
    )
    row_delta = jnp.sum(probs * d_probs, axis=-1, keepdims=True)
    d_scores = (probs * (d_probs - row_delta)).astype(jnp.bfloat16)
    query_gradient = jnp.einsum(
        "kgts,skd->tkgd", d_scores, key_reduced, preferred_element_type=jnp.float32
    ) * HEAD_SIZE ** (-0.5)
    key_gradient = jnp.einsum(
        "kgts,tkgd->skd", d_scores, query_rows, preferred_element_type=jnp.float32
    ) * HEAD_SIZE ** (-0.5)
    (query_key_gradient,) = rope_back(
        jnp.concatenate(
            [
                query_gradient.reshape(count_of_rows, QUERY_HEADS * HEAD_SIZE),
                key_gradient.reshape(count_of_rows, KEY_VALUE_HEADS * HEAD_SIZE),
            ],
            axis=1,
        )
    )
    d_projected = jnp.concatenate(
        [
            mixer_projection_gradient,
            query_key_gradient,
            value_gradient.reshape(count_of_rows, KEY_VALUE_HEADS * HEAD_SIZE),
        ],
        axis=1,
    ).astype(jnp.bfloat16)
    d_main = jnp.concatenate(
        [d_projected[:, : MIXER_WIDTH + CONV], d_projected[:, split_boundary:]], axis=1
    )
    d_dt = d_projected[:, MIXER_WIDTH + CONV : split_boundary]
    grad_in = left_product(normed, d_main)
    grad_dt = left_product(normed, d_dt)
    d_normed = right_product(d_main, back_in) + right_product(d_dt, back_dt)
    d_inputs, d_gain_one = norm_back(d_normed)
    token_grad = (d_hidden + d_inputs).astype(jnp.bfloat16)
    grad_gains = jnp.concatenate([d_gain_one, d_gain_two, d_gain_mix], axis=0)
    owned_in, owned_out, owned_gu, owned_down, owned_dt, owned_gains, owned_conv = (
        lax.psum_scatter(grad_in, "shard", scatter_dimension=0, tiled=True),
        lax.psum_scatter(grad_out, "shard", scatter_dimension=0, tiled=True),
        lax.psum_scatter(grad_gu, "shard", scatter_dimension=0, tiled=True),
        lax.psum_scatter(grad_down, "shard", scatter_dimension=0, tiled=True),
        lax.psum_scatter(grad_dt, "shard", scatter_dimension=0, tiled=True),
        lax.psum_scatter(grad_gains, "shard", scatter_dimension=0, tiled=True),
        lax.psum_scatter(d_conv, "shard", scatter_dimension=1, tiled=True),
    )
    summed_in, summed_out, summed_gu, summed_down = (
        lax.psum_scatter(owned_in, "rep", scatter_dimension=1, tiled=True),
        lax.psum_scatter(owned_out, "rep", scatter_dimension=1, tiled=True),
        lax.psum_scatter(owned_gu, "rep", scatter_dimension=1, tiled=True),
        lax.psum_scatter(owned_down, "rep", scatter_dimension=1, tiled=True),
    )
    summed_dt, summed_gains, summed_conv = lax.psum((owned_dt, owned_gains, owned_conv), "rep")
    ssm_total = lax.psum(d_ssm, ("rep", "shard"))
    rep_index = lax.axis_index("rep")
    in_piece = column_block(in_proj, in_proj_first, rep_index)
    out_piece = column_block(out_proj, out_proj_first, rep_index)
    gu_piece = column_block(gate_up, gate_up_first, rep_index)
    down_piece = column_block(down_proj, down_proj_first, rep_index)
    in_first_new, in_second_new, in_piece_new = adam_update(
        in_piece, in_proj_first, in_proj_second, summed_in / token_count, 0.7 * D ** (-0.5), 0.1
    )
    out_first_new, out_second_new, out_piece_new = adam_update(
        out_piece,
        out_proj_first,
        out_proj_second,
        summed_out / token_count,
        0.7 * NOUT ** (-0.5),
        0.1,
    )
    gu_first_new, gu_second_new, gu_piece_new = adam_update(
        gu_piece, gate_up_first, gate_up_second, summed_gu / token_count, 0.7 * D ** (-0.5), 0.1
    )
    down_first_new, down_second_new, down_piece_new = adam_update(
        down_piece,
        down_proj_first,
        down_proj_second,
        summed_down / token_count,
        0.7 * FF ** (-0.5),
        0.1,
    )
    in_new, out_new, gu_new, down_new = (
        lax.all_gather(in_piece_new, "rep", axis=1, tiled=True),
        lax.all_gather(out_piece_new, "rep", axis=1, tiled=True),
        lax.all_gather(gu_piece_new, "rep", axis=1, tiled=True),
        lax.all_gather(down_piece_new, "rep", axis=1, tiled=True),
    )
    dt_first_new, dt_second_new, dt_new = adam_update(
        dt_proj, dt_proj_first, dt_proj_second, summed_dt / token_count, 0.7 * D ** (-0.5), 0.1
    )
    gain_first_new, gain_second_new, gain_new = adam_update(
        norm_gains, gains_first, gains_second, summed_gains / token_count, 0.3, 0.0
    )
    conv_first_new, conv_second_new, conv_new = adam_update(
        conv_taps, conv_first, conv_second, summed_conv / token_count, 0.3, 0.1
    )
    ssm_first_new, ssm_second_new, ssm_new = adam_update(
        ssm_params, ssm_first, ssm_second, ssm_total / token_count, 0.8, 0.0
    )
    return (
        output.astype(jnp.bfloat16),
        token_grad,
        in_first_new,
        in_second_new,
        in_new,
        dt_first_new,
        dt_second_new,
        dt_new,
        out_first_new,
        out_second_new,
        out_new,
        gu_first_new,
        gu_second_new,
        gu_new,
        down_first_new,
        down_second_new,
        down_new,
        gain_first_new,
        gain_second_new,
        gain_new,
        conv_first_new,
        conv_second_new,
        conv_new,
        ssm_first_new,
        ssm_second_new,
        ssm_new,
    )


def solution(mesh):
    in_specs = (
        P(("rep", "shard"), None),
        P(("rep", "shard"), None),
        P(("rep", "shard")),
        P("shard", None),
        P("shard", "rep"),
        P("shard", "rep"),
        P("shard", None),
        P("shard", None),
        P("shard", None),
        P("shard", None),
        P("shard", "rep"),
        P("shard", "rep"),
        P("shard", None),
        P("shard", "rep"),
        P("shard", "rep"),
        P("shard", None),
        P("shard", "rep"),
        P("shard", "rep"),
        P("shard"),
        P("shard"),
        P("shard"),
        P(None, "shard"),
        P(None, "shard"),
        P(None, "shard"),
        P(),
        P(),
        P(),
    )
    out_specs = (
        P(("rep", "shard"), None),
        P(("rep", "shard"), None),
        P("shard", "rep"),
        P("shard", "rep"),
        P("shard", None),
        P("shard", None),
        P("shard", None),
        P("shard", None),
        P("shard", "rep"),
        P("shard", "rep"),
        P("shard", None),
        P("shard", "rep"),
        P("shard", "rep"),
        P("shard", None),
        P("shard", "rep"),
        P("shard", "rep"),
        P("shard", None),
        P("shard"),
        P("shard"),
        P("shard"),
        P(None, "shard"),
        P(None, "shard"),
        P(None, "shard"),
        P(),
        P(),
        P(),
    )
    return jax.shard_map(local, mesh=mesh, in_specs=in_specs, out_specs=out_specs, check_vma=False)
```

profile of v0, /device:TPU:0, one launch (start us, length us, event | category | flops | bytes accessed | tf_op | source)
XLA Modules:
  0.0 1217.0 jit_solution(1349117939348930481)
XLA Ops:
  20.5 9.8 all-gather.1
  31.4 9.0 all_gather.41
  42.3 7.3 all-gather
  52.4 49.6 %all-gather.11.cloned.1.call-done = bf16[1024,4096]{1,0:T(8,128)(2,1)} async-done(((bf16[256,4096]{1,0:T(8,128)(2,1)}), bf16[1024,4096]{1,0:T(8,128)(2,1)}) %all-gather.11.cloned.1.call-update) | async-done | bytes 8388624 | tf_op jit(solution)/shard_map/all_gather | solution.py:183
  102.0 4.7 fusion.121
  119.5 5.5 fusion.15
  132.2 25.0 %all-gather.13.cloned.1.call-done = bf16[2048,1024]{1,0:T(8,128)(2,1)} async-done(((bf16[512,1024]{1,0:T(8,128)(2,1)}), bf16[2048,1024]{1,0:T(8,128)(2,1)}) %all-gather.13.cloned.1.call-update) | async-done | bytes 4194320 | tf_op jit(solution)/shard_map/all_gather | solution.py:185
  161.4 85.8 %all-gather.15.cloned.1.call-done = bf16[1024,4096]{1,0:T(8,128)(2,1)} async-done(((bf16[256,4096]{1,0:T(8,128)(2,1)}), bf16[1024,4096]{1,0:T(8,128)(2,1)}) %all-gather.15.cloned.1.call-update) | async-done | bytes 8388624 | tf_op jit(solution)/shard_map/all_gather | solution.py:186
  247.3 6.0 fusion.116
  253.3 49.0 %all-gather.17.cloned.1.call-done = bf16[2048,1024]{1,0:T(8,128)(2,1)} async-done(((bf16[512,1024]{1,0:T(8,128)(2,1)}), bf16[2048,1024]{1,0:T(8,128)(2,1)}) %all-gather.17.cloned.1.call-update) | async-done | bytes 4194320 | tf_op jit(solution)/shard_map/all_gather | solution.py:187
  302.3 6.0 fusion.75
  309.1 4.9 fusion.76
  314.1 7.7 multiply_reduce_fusion.10
  327.5 10.1 fusion.70
  351.1 5.7 fusion.28
  382.3 9.8 fusion.62
  392.1 8.5 reduce-scatter.27.cloned.1.call-done
  400.7 89.6 %reduce-scatter.19.cloned.1.call-done = f32[512,1024]{1,0:T(8,128)} async-done(((f32[2048,1024]{1,0:T(8,128)}), f32[512,1024]{1,0:T(8,128)}) %reduce-scatter.19.cloned.1.call-update) | async-done | bytes 2097168 | tf_op jit(solution)/shard_map/reduce_scatter | solution.py:322
  490.3 156.9 %reduce-scatter.23.cloned.1.call-done = f32[256,4096]{1,0:T(8,128)} async-done(((f32[1024,4096]{1,0:T(8,128)}), f32[256,4096]{1,0:T(8,128)}) %reduce-scatter.23.cloned.1.call-update) | async-done | bytes 4194320 | tf_op jit(solution)/shard_map/reduce_scatter | solution.py:323
  647.2 156.9 %reduce-scatter.13.cloned.1.call-done = f32[256,4096]{1,0:T(8,128)} async-done(((f32[1024,4096]{1,0:T(8,128)}), f32[256,4096]{1,0:T(8,128)}) %reduce-scatter.13.cloned.1.call-update) | async-done | bytes 4194320 | tf_op jit(solution)/shard_map/reduce_scatter | solution.py:321
  808.3 40.0 %all-reduce.25 = (f32[]{:T(128)}, f32[3,24]{1,0:T(4,128)S(1)}) all-reduce(f32[]{:T(128)S(6)} %convert_element_type.132, f32[3,24]{1,0:T(4,128)S(1)} %pad_add_fusion.2), channel_id=1, replica_groups=mesh['rep'=8,'shard'=4] {'rep','shard'}, use_global_device_ids=true, to_apply=%region_21.22 | all-reduce | flops 73 | bytes 584 | tf_op jit(solution)/shard_map/psum | solution.py:181
  851.3 27.9 %reduce-scatter.21.cloned.1.call-done = f32[512,128]{1,0:T(8,128)} async-done(((f32[512,1024]{1,0:T(8,128)}), f32[512,128]{1,0:T(8,128)}) %reduce-scatter.21.cloned.1.call-update) | async-done | bytes 262160 | tf_op jit(solution)/shard_map/reduce_scatter | solution.py:331
  882.0 48.3 %reduce-scatter.25.cloned.1.call-done = f32[256,512]{1,0:T(8,128)} async-done(((f32[256,4096]{1,0:T(8,128)}), f32[256,512]{1,0:T(8,128)}) %reduce-scatter.25.cloned.1.call-update) | async-done | bytes 524304 | tf_op jit(solution)/shard_map/reduce_scatter | solution.py:332
  933.6 47.0 %reduce-scatter.15.cloned.1.call-done = f32[256,512]{1,0:T(8,128)} async-done(((f32[256,4096]{1,0:T(8,128)}), f32[256,512]{1,0:T(8,128)}) %reduce-scatter.15.cloned.1.call-update) | async-done | bytes 524304 | tf_op jit(solution)/shard_map/reduce_scatter | solution.py:330
  985.5 6.4 fusion.63
  992.3 16.0 %all-reduce.24 = f32[3584]{0:T(1024)S(1)} all-reduce(f32[3584]{0:T(1024)S(1)} %pad_maximum_fusion.7), channel_id=11, replica_groups=mesh['rep'=8,'shard'=4] {'shard'}, use_global_device_ids=true, to_apply=%region_33.34.clone | all-reduce | flops 3584 | bytes 28672
  1015.3 20.3 %reduce-scatter.17.cloned.1.call-done = f32[256,24]{0,1:T(8,128)} async-done(((f32[1024,24]{0,1:T(8,128)}), f32[256,24]{0,1:T(8,128)}) %reduce-scatter.17.cloned.1.call-update) | async-done | bytes 24592 | tf_op jit(solution)/shard_map/reduce_scatter | solution.py:325
  1035.7 29.4 %all-reduce.26 = (f32[256,24]{0,1:T(8,128)S(1)}, f32[896]{0:T(1024)S(1)}, f32[5,448]{1,0:T(8,128)S(1)}) all-reduce(f32[256,24]{0,1:T(8,128)} %reduce-scatter.17.cloned.1.call-done, f32[896]{0:T(1024)S(1)} %dynamic-slice.1, f32[5,448]{1,0:T(8,128)S(1)} %copy.165), channel_id=1, replica_groups=mesh['rep'=8,'shard'=4] {'rep'}, use_global_device_ids=true, to_apply=%region_23.24 | all-reduce | flops 9280 | bytes 74240 | tf_op jit(solution)/shard_map/psum | solution.py:335
  1070.2 31.3 %all-gather.21.cloned.1.call-done = f32[512,1024]{1,0:T(8,128)} async-done(((f32[512,128]{1,0:T(8,128)}), f32[512,1024]{1,0:T(8,128)}) %all-gather.21.cloned.1.call-update) | async-done | bytes 2097168 | tf_op jit(solution)/shard_map/all_gather | solution.py:366
  1101.4 48.4 %all-gather.23.cloned.1.call-done = f32[256,4096]{1,0:T(8,128)} async-done(((f32[256,512]{1,0:T(8,128)}), f32[256,4096]{1,0:T(8,128)}) %all-gather.23.cloned.1.call-update) | async-done | bytes 4194320 | tf_op jit(solution)/shard_map/all_gather | solution.py:367
  1149.8 48.0 %all-gather.19.cloned.1.call-done = f32[256,4096]{1,0:T(8,128)} async-done(((f32[256,512]{1,0:T(8,128)}), f32[256,4096]{1,0:T(8,128)}) %all-gather.19.cloned.1.call-update) | async-done | bytes 4194320 | tf_op jit(solution)/shard_map/all_gather | solution.py:365
  1197.8 4.8 copy.170
  (390 shorter events, 124.1 us)
Async XLA Ops:
  7.2 94.8 %all-gather.11.cloned.1.call-start = ((), (), s32[]{:S(2)}) async-start(), calls=%async_computation.10 | async-start | bytes 10485760 | tf_op jit(solution)/shard_map/all_gather | solution.py:183
  11.1 146.1 %all-gather.13.cloned.1.call-start = ((), (), s32[]{:S(2)}) async-start(), calls=%async_computation.11 | async-start | bytes 5242880 | tf_op jit(solution)/shard_map/all_gather | solution.py:185
  13.8 233.5 %all-gather.15.cloned.1.call-start = ((), (), s32[]{:S(2)}) async-start(), calls=%async_computation.12 | async-start | bytes 10485760 | tf_op jit(solution)/shard_map/all_gather | solution.py:186
  17.7 284.5 %all-gather.17.cloned.1.call-start = ((), (), s32[]{:S(2)}) async-start(), calls=%async_computation.13 | async-start | bytes 5242880 | tf_op jit(solution)/shard_map/all_gather | solution.py:187
  20.4 380.2 %reduce-scatter.27.cloned.1.call-start = ((), (), s32[]{:S(2)}) async-start(), calls=%async_computation.24 | async-start | bytes 10485760 | tf_op jit(solution)/shard_map/reduce_scatter | solution.py:324
  30.5 76.3 %copy-start.65 = (f32[128]{0:T(128)}, f32[128]{0:T(128)S(1)}, u32[]{:S(2)}) copy-start(f32[128]{0:T(128)S(1)} %fusion.104) | copy-start | bytes 1540
  31.4 88.1 %copy-start.103 = (f32[24]{0:T(128)}, f32[24]{0:T(128)S(1)}, u32[]{:S(2)}) copy-start(f32[24]{0:T(128)S(1)} %get-tuple-element.97) | copy-start | bytes 292
  41.6 65.1 %copy-start.42 = (pred[128,128]{0,1:T(8,128)(4,1)}, pred[128,128]{0,1:T(8,128)(4,1)S(1)}, u32[]{:S(2)}) copy-start(pred[128,128]{0,1:T(8,128)(4,1)S(1)} %fusion.91) | copy-start | bytes 49156
  49.9 69.6 %copy-start.76 = (f32[24,128]{1,0:T(8,128)}, f32[24,128]{1,0:T(8,128)S(1)}, u32[]{:S(2)}) copy-start(f32[24,128]{1,0:T(8,128)S(1)} %copy.132) | copy-start | bytes 36868
  50.0 69.5 %copy-start.77 = (f32[24,128]{1,0:T(8,128)}, f32[24,128]{1,0:T(8,128)S(1)}, u32[]{:S(2)}) copy-start(f32[24,128]{1,0:T(8,128)S(1)} %copy.134) | copy-start | bytes 36868
  50.1 69.4 %copy-start.75 = (pred[128,128]{1,0:T(8,128)(4,1)}, pred[128,128]{1,0:T(8,128)(4,1)S(1)}, u32[]{:S(2)}) copy-start(pred[128,128]{1,0:T(8,128)(4,1)S(1)} %copy.130) | copy-start | bytes 49156
  50.9 59.3 %copy-start.84 = (pred[128]{0:T(512)(128)(4,1)}, pred[128]{0:T(512)(128)(4,1)S(1)}, u32[]{:S(2)}) copy-start(pred[128]{0:T(512)(128)(4,1)S(1)} %get-tuple-element.84) | copy-start | bytes 388
  52.2 58.0 %copy-start.48 = (f32[1792]{0:T(1024)}, f32[1792]{0:T(1024)S(1)}, u32[]{:S(2)}) copy-start(f32[1792]{0:T(1024)S(1)} %get-tuple-element.42) | copy-start | bytes 21508
  52.2 58.0 %copy-start.50 = (f32[1792]{0:T(1024)}, f32[1792]{0:T(1024)S(1)}, u32[]{:S(2)}) copy-start(f32[1792]{0:T(1024)S(1)} %get-tuple-element.45) | copy-start | bytes 21508
  52.2 58.0 %copy-start.52 = (f32[1792]{0:T(1024)}, f32[1792]{0:T(1024)S(1)}, u32[]{:S(2)}) copy-start(f32[1792]{0:T(1024)S(1)} %get-tuple-element.43) | copy-start | bytes 21508
  314.0 176.2 %reduce-scatter.19.cloned.1.call-start = ((), (), s32[]{:S(2)}) async-start(), calls=%async_computation.18 | async-start | bytes 10485760 | tf_op jit(solution)/shard_map/reduce_scatter | solution.py:322
  327.4 319.7 %reduce-scatter.23.cloned.1.call-start = ((), (), s32[]{:S(2)}) async-start(), calls=%async_computation.21 | async-start | bytes 20971520 | tf_op jit(solution)/shard_map/reduce_scatter | solution.py:323
  337.6 466.5 %reduce-scatter.13.cloned.1.call-start = ((), (), s32[]{:S(2)}) async-start(), calls=%async_computation.14 | async-start | bytes 20971520 | tf_op jit(solution)/shard_map/reduce_scatter | solution.py:321
  392.1 456.3 %reduce-scatter.29.cloned.1.call-start = ((), (), s32[]{:S(2)}) async-start(), calls=%async_computation.25 | async-start | bytes 2359296 | tf_op jit(solution)/shard_map/reduce_scatter | solution.py:333
  400.6 478.6 %reduce-scatter.21.cloned.1.call-start = ((), (), s32[]{:S(2)}) async-start(), calls=%async_computation.19 | async-start | bytes 2359296 | tf_op jit(solution)/shard_map/reduce_scatter | solution.py:331
  490.3 440.0 %reduce-scatter.25.cloned.1.call-start = ((), (), s32[]{:S(2)}) async-start(), calls=%async_computation.22 | async-start | bytes 4718592 | tf_op jit(solution)/shard_map/reduce_scatter | solution.py:332
  647.2 333.4 %reduce-scatter.15.cloned.1.call-start = ((), (), s32[]{:S(2)}) async-start(), calls=%async_computation.15 | async-start | bytes 4718592 | tf_op jit(solution)/shard_map/reduce_scatter | solution.py:330
  804.2 210.1 %reduce-scatter.31.cloned.1.call-start = ((), (), s32[]{:S(2)}) async-start(), calls=%async_computation.27 | async-start | bytes 1146880
  806.5 72.7 %copy-start.33 = (f32[512,128]{1,0:T(8,128)S(1)}, f32[512,128]{1,0:T(8,128)}, u32[]{:S(2)}) copy-start(f32[512,128]{1,0:T(8,128)} %param.38) | copy-start | bytes 786436
  806.5 72.7 %copy-start.34 = (f32[512,128]{1,0:T(8,128)S(1)}, f32[512,128]{1,0:T(8,128)}, u32[]{:S(2)}) copy-start(f32[512,128]{1,0:T(8,128)} %param.37) | copy-start | bytes 786436
  807.3 228.3 %reduce-scatter.17.cloned.1.call-start = ((), (), s32[]{:S(2)}) async-start(), calls=%async_computation.17 | async-start | bytes 122880 | tf_op jit(solution)/shard_map/reduce_scatter | solution.py:325
  848.3 221.9 %all-gather.25.cloned.1.call-start = ((), (), s32[]{:S(2)}) async-start(), calls=%async_computation.26 | async-start | bytes 2359296 | tf_op jit(solution)/shard_map/all_gather | solution.py:368
  848.4 81.9 %copy-start.26 = (f32[256,512]{1,0:T(8,128)S(1)}, f32[256,512]{1,0:T(8,128)}, u32[]{:S(2)}) copy-start(f32[256,512]{1,0:T(8,128)} %param.41) | copy-start | bytes 1572868
  848.4 81.9 %copy-start.27 = (f32[256,512]{1,0:T(8,128)S(1)}, f32[256,512]{1,0:T(8,128)}, u32[]{:S(2)}) copy-start(f32[256,512]{1,0:T(8,128)} %param.40) | copy-start | bytes 1572868
  851.3 250.1 %all-gather.21.cloned.1.call-start = ((), (), s32[]{:S(2)}) async-start(), calls=%async_computation.20 | async-start | bytes 2359296 | tf_op jit(solution)/shard_map/all_gather | solution.py:366
  881.9 267.9 %all-gather.23.cloned.1.call-start = ((), (), s32[]{:S(2)}) async-start(), calls=%async_computation.23 | async-start | bytes 4718592 | tf_op jit(solution)/shard_map/all_gather | solution.py:367
  933.6 264.2 %all-gather.19.cloned.1.call-start = ((), (), s32[]{:S(2)}) async-start(), calls=%async_computation.16 | async-start | bytes 4718592 | tf_op jit(solution)/shard_map/all_gather | solution.py:365
  (94 other events, 1384.2 us)
Sparse Core Ops, SparseCore 0:
  11.2 90.8 all-gather.10
  104.5 52.6 all-gather.12
  159.6 87.5 all-gather.14
  249.5 52.6 all-gather.16
  314.1 86.4 reduce-scatter.26
  403.8 86.3 reduce-scatter.18
  493.3 153.8 reduce-scatter.22
  650.2 153.8 reduce-scatter.12
  806.4 36.2 reduce-scatter.28
  844.8 34.3 reduce-scatter.20
  881.5 48.6 reduce-scatter.24
  932.4 48.1 reduce-scatter.14
  984.1 25.0 reduce-scatter.30
  1011.8 23.7 reduce-scatter.16
  1037.2 32.9 all-gather.24
  1071.7 29.6 all-gather.20
  1103.5 46.2 all-gather.22
  1151.9 45.8 all-gather.18
where the time goes:
time: 1230 us; the launch traced here: 1220 us
  waiting for transfers between devices  894 us (73%)
  blocking collectives  111 us (9%)
  matrix products  92.7 us (8%)
  other arithmetic  53.4 us (4%)
  local copies, waits for them, and re-layouts  47.2 us (4%)
  between operations  17.5 us (1%)
    reduce_scatter x1, waiting for transfers between devices, local(): lax.psum_scatter(grad_in, 'shard', scatter_dimension=0, tiled=True)  157 us
    reduce_scatter x1, waiting for transfers between devices, local(): lax.psum_scatter(grad_gu, 'shard', scatter_dimension=0, tiled=True)  157 us
    reduce_scatter x1, waiting for transfers between devices, local(): lax.psum_scatter(grad_out, 'shard', scatter_dimension=0, tiled=True)  89.6 us
    all_gather x1, waiting for transfers between devices, local(): lax.all_gather(gate_up.astype(jnp.bfloat16), 'shard', axis=0, tiled=True)  85.8 us
    all_gather x1, waiting for transfers between devices, local(): lax.all_gather(in_proj.astype(jnp.bfloat16), 'shard', axis=0, tiled=True)  49.6 us
    all_gather x1, waiting for transfers between devices, local(): lax.all_gather(down_proj.astype(jnp.bfloat16), 'shard', axis=0, tiled=True)  49 us
    all_gather x1, waiting for transfers between devices, local(): lax.all_gather(gu_piece_new, 'rep', axis=1, tiled=True)  48.4 us
    reduce_scatter x1, waiting for transfers between devices, local(): lax.psum_scatter(owned_gu, 'rep', scatter_dimension=1, tiled=True)  48.3 us
  transfers between devices with their start and end apart: 18, of which 16 were waited for; matrix products, arithmetic and copies ran while one was open for 13% of the time, Pallas kernels for 0%

commit v1 on v0

--- a/solution.py
+++ b/solution.py
@@ -1,3 +1,5 @@
+import functools
+
 import jax
 import jax.numpy as jnp
 from jax import lax
@@ -143,12 +145,78 @@
     return (new_first, new_second, new_param)
 
 
+def core_halves(columns, core):
+    half = columns.shape[1] // 2
+    return (
+        lax.dynamic_slice_in_dim(columns, core * half, half, 1),
+        lax.dynamic_slice_in_dim(columns, (1 - core) * half, half, 1),
+    )
+
+
+def swap_cores(values, reps):
+    return lax.ppermute(values, "rep", [(r, r ^ 1) for r in range(reps)])
+
+
+def gather_weight(weight, core, reps):
+    mine, _ = core_halves(weight.astype(jnp.bfloat16), core)
+    mine = lax.all_gather(mine, "shard", axis=0, tiled=True)
+    return (mine, swap_cores(mine, reps))
+
+
+def forward_product(left, pair, core):
+    own = jnp.dot(left, pair[0], preferred_element_type=jnp.float32)
+    other = jnp.dot(left, pair[1], preferred_element_type=jnp.float32)
+    low = jnp.where(core == 0, own, other)
+    high = jnp.where(core == 0, other, own)
+    return jnp.concatenate([low, high], axis=1)
+
+
+def backward_product(left, pair, core):
+    own, other = core_halves(left, core)
+    return right_product(own, pair[0]) + right_product(other, pair[1])
+
+
+def pair_rows(values, reps):
+    return jnp.concatenate([values, swap_cores(values, reps)], axis=0)
+
+
+def pair_columns(values, core, reps):
+    count_of_rows, width = values.shape
+    blocks = values.reshape(count_of_rows, reps // 2, 2, width // reps)
+    own = lax.dynamic_index_in_dim(blocks, core, 2, False).reshape(count_of_rows, width // 2)
+    other = lax.dynamic_index_in_dim(blocks, 1 - core, 2, False).reshape(count_of_rows, width // 2)
+    return jnp.concatenate([own, swap_cores(other, reps)], axis=0)
+
+
+def summed_block(left, right, core, reps):
+    grad = left_product(pair_rows(left, reps), pair_columns(right, core, reps))
+    owned = lax.psum_scatter(
+        grad.astype(jnp.bfloat16), "shard", scatter_dimension=0, tiled=True
+    )
+    groups = [list(range(c, reps, 2)) for c in range(2)]
+    block = lax.psum_scatter(
+        owned, "rep", scatter_dimension=1, axis_index_groups=groups, tiled=True
+    )
+    return block.astype(jnp.float32)
+
+
+def adam_delta(param, first, second, grad, rate, decay):
+    new_first, new_second, delta = adam_update(param, first, second, grad, rate, decay)
+    return (new_first, new_second, (delta - param).astype(jnp.bfloat16))
+
+
+def gathered_weight(weight, delta):
+    return weight + lax.all_gather(delta, "rep", axis=1, tiled=True).astype(jnp.float32)
+
+
 def column_block(whole_rows, like, block_index):
     width = like.shape[1]
     return lax.dynamic_slice_in_dim(whole_rows, block_index * width, width, 1)
 
 
 def local(
+    reps,
+    shards,
     tokens,
     cotangent,
     seq_len,
@@ -177,17 +245,29 @@
     ssm_first,
     ssm_second,
 ):
+    rep_index = lax.axis_index("rep")
+    shard_index = lax.axis_index("shard")
+    core = lax.rem(rep_index, 2)
     token_local = jnp.sum(seq_len).astype(jnp.float32)
     token_count = lax.psum(token_local, ("rep", "shard"))
-    full_in, full_dt, full_out, full_gu, full_down, full_gains, full_conv = (
-        lax.all_gather(in_proj.astype(jnp.bfloat16), "shard", axis=0, tiled=True),
-        lax.all_gather(dt_proj.astype(jnp.bfloat16), "shard", axis=0, tiled=True),
-        lax.all_gather(out_proj.astype(jnp.bfloat16), "shard", axis=0, tiled=True),
-        lax.all_gather(gate_up.astype(jnp.bfloat16), "shard", axis=0, tiled=True),
-        lax.all_gather(down_proj.astype(jnp.bfloat16), "shard", axis=0, tiled=True),
-        lax.all_gather(norm_gains.astype(jnp.bfloat16), "shard", axis=0, tiled=True),
-        lax.all_gather(conv_taps.astype(jnp.bfloat16), "shard", axis=1, tiled=True),
-    )
+    small = jnp.concatenate(
+        [dt_proj.reshape(-1), norm_gains.reshape(-1), conv_taps.reshape(-1)]
+    ).astype(jnp.bfloat16)
+    small = lax.all_gather(small, "shard", axis=0)
+    dt_size, gain_size = dt_proj.size, norm_gains.size
+    full_dt = small[:, :dt_size].reshape(D, MIXER_HEADS)
+    full_gains = small[:, dt_size : dt_size + gain_size].reshape(-1)
+    full_conv = (
+        small[:, dt_size + gain_size :]
+        .reshape(shards, KCONV + 1, CONV // shards)
+        .transpose(1, 0, 2)
+        .reshape(KCONV + 1, CONV)
+    )
+    full_in = gather_weight(in_proj, core, reps)
+    full_out = gather_weight(out_proj, core, reps)
+    full_gu = gather_weight(gate_up, core, reps)
+    full_down = gather_weight(down_proj, core, reps)
+    tokens, token_count = lax.optimization_barrier((tokens, token_count))
     count_of_rows = tokens.shape[0]
     row_alive, token_position, pair_mask = layout(seq_len, count_of_rows)
     inputs = tokens.astype(jnp.float32)
@@ -195,7 +275,7 @@
     conv_full = full_conv.astype(jnp.float32)
     normed_value, norm_back = jax.vjp(rms_scale, inputs, gains_full[:D])
     normed = normed_value.astype(jnp.bfloat16)
-    main_proj = jnp.dot(normed, full_in, preferred_element_type=jnp.float32)
+    main_proj = forward_product(normed, full_in, core)
     dt_raw = jnp.dot(normed, full_dt, preferred_element_type=jnp.float32)
     projected_input = jnp.concatenate(
         [main_proj[:, : MIXER_WIDTH + CONV], dt_raw, main_proj[:, MIXER_WIDTH + CONV :]], axis=1
@@ -241,34 +321,27 @@
     )
     attended_low = attended.reshape(count_of_rows, QUERY_HEADS * HEAD_SIZE).astype(jnp.bfloat16)
     branch_in = jnp.concatenate([mixer_low, attended_low * ATT_MULT], axis=1)
-    branch = jnp.dot(branch_in, full_out, preferred_element_type=jnp.float32)
+    branch = forward_product(branch_in, full_out, core)
     hidden = inputs + branch
     normed_two_value, norm_two_back = jax.vjp(rms_scale, hidden, gains_full[D : 2 * D])
     normed_two = normed_two_value.astype(jnp.bfloat16)
-    gate_vals = jnp.dot(normed_two, full_gu, preferred_element_type=jnp.float32)
+    gate_vals = forward_product(normed_two, full_gu, core)
     act_value, swiglu_back = jax.vjp(swiglu, gate_vals)
     act_low = act_value.astype(jnp.bfloat16)
-    output = hidden + jnp.dot(act_low, full_down, preferred_element_type=jnp.float32)
-    back_in, back_dt, back_out, back_gu, back_down = (
-        lax.all_gather(in_proj.astype(jnp.bfloat16), "shard", axis=0, tiled=True),
-        lax.all_gather(dt_proj.astype(jnp.bfloat16), "shard", axis=0, tiled=True),
-        lax.all_gather(out_proj.astype(jnp.bfloat16), "shard", axis=0, tiled=True),
-        lax.all_gather(gate_up.astype(jnp.bfloat16), "shard", axis=0, tiled=True),
-        lax.all_gather(down_proj.astype(jnp.bfloat16), "shard", axis=0, tiled=True),
-    )
+    output = hidden + forward_product(act_low, full_down, core)
     upstream = cotangent.astype(jnp.float32) * row_alive[:, None].astype(jnp.float32)
     upstream_low = upstream.astype(jnp.bfloat16)
-    grad_down = left_product(act_low, upstream_low)
-    d_act = right_product(upstream_low, back_down)
+    summed_down = summed_block(act_low, upstream_low, core, reps)
+    d_act = backward_product(upstream_low, full_down, core)
     (d_gate_vals,) = swiglu_back(d_act)
     d_gate_low = d_gate_vals.astype(jnp.bfloat16)
-    grad_gu = left_product(normed_two, d_gate_low)
-    d_normed_two = right_product(d_gate_low, back_gu)
+    summed_gu = summed_block(normed_two, d_gate_low, core, reps)
+    d_normed_two = backward_product(d_gate_low, full_gu, core)
     d_hidden_norm, d_gain_two = norm_two_back(d_normed_two)
     d_hidden = upstream + d_hidden_norm
     d_branch_low = d_hidden.astype(jnp.bfloat16)
-    grad_out = left_product(branch_in, d_branch_low)
-    d_branch_in = right_product(d_branch_low, back_out)
+    summed_out = summed_block(branch_in, d_branch_low, core, reps)
+    d_branch_in = backward_product(d_branch_low, full_out, core)
     mixer_projection_gradient, d_conv, d_ssm, d_gain_mix = mixer_back(d_branch_in[:, :MIXER_WIDTH])
     d_attended = (
         (d_branch_in[:, MIXER_WIDTH:] * ATT_MULT)
@@ -311,38 +384,41 @@
         [d_projected[:, : MIXER_WIDTH + CONV], d_projected[:, split_boundary:]], axis=1
     )
     d_dt = d_projected[:, MIXER_WIDTH + CONV : split_boundary]
-    grad_in = left_product(normed, d_main)
+    summed_in = summed_block(normed, d_main, core, reps)
     grad_dt = left_product(normed, d_dt)
-    d_normed = right_product(d_main, back_in) + right_product(d_dt, back_dt)
+    d_normed = backward_product(d_main, full_in, core) + right_product(d_dt, full_dt)
     d_inputs, d_gain_one = norm_back(d_normed)
     token_grad = (d_hidden + d_inputs).astype(jnp.bfloat16)
     grad_gains = jnp.concatenate([d_gain_one, d_gain_two, d_gain_mix], axis=0)
-    owned_in, owned_out, owned_gu, owned_down, owned_dt, owned_gains, owned_conv = (
-        lax.psum_scatter(grad_in, "shard", scatter_dimension=0, tiled=True),
-        lax.psum_scatter(grad_out, "shard", scatter_dimension=0, tiled=True),
-        lax.psum_scatter(grad_gu, "shard", scatter_dimension=0, tiled=True),
-        lax.psum_scatter(grad_down, "shard", scatter_dimension=0, tiled=True),
-        lax.psum_scatter(grad_dt, "shard", scatter_dimension=0, tiled=True),
-        lax.psum_scatter(grad_gains, "shard", scatter_dimension=0, tiled=True),
-        lax.psum_scatter(d_conv, "shard", scatter_dimension=1, tiled=True),
-    )
-    summed_in, summed_out, summed_gu, summed_down = (
-        lax.psum_scatter(owned_in, "rep", scatter_dimension=1, tiled=True),
-        lax.psum_scatter(owned_out, "rep", scatter_dimension=1, tiled=True),
-        lax.psum_scatter(owned_gu, "rep", scatter_dimension=1, tiled=True),
-        lax.psum_scatter(owned_down, "rep", scatter_dimension=1, tiled=True),
-    )
-    summed_dt, summed_gains, summed_conv = lax.psum((owned_dt, owned_gains, owned_conv), "rep")
-    ssm_total = lax.psum(d_ssm, ("rep", "shard"))
-    rep_index = lax.axis_index("rep")
+    small_sum = lax.psum(
+        jnp.concatenate(
+            [grad_dt.reshape(-1), grad_gains, d_conv.reshape(-1), d_ssm.reshape(-1)]
+        ),
+        ("rep", "shard"),
+    )
+    cut_dt = grad_dt.size
+    cut_gains = cut_dt + grad_gains.size
+    cut_conv = cut_gains + d_conv.size
+    summed_dt = lax.dynamic_slice_in_dim(small_sum[:cut_dt], shard_index * dt_size, dt_size, 0)
+    summed_dt = summed_dt.reshape(dt_proj.shape)
+    summed_gains = lax.dynamic_slice_in_dim(
+        small_sum[cut_dt:cut_gains], shard_index * gain_size, gain_size, 0
+    )
+    summed_conv = lax.dynamic_slice_in_dim(
+        small_sum[cut_gains:cut_conv].reshape(d_conv.shape),
+        shard_index * conv_taps.shape[1],
+        conv_taps.shape[1],
+        1,
+    )
+    ssm_total = small_sum[cut_conv:].reshape(d_ssm.shape)
     in_piece = column_block(in_proj, in_proj_first, rep_index)
     out_piece = column_block(out_proj, out_proj_first, rep_index)
     gu_piece = column_block(gate_up, gate_up_first, rep_index)
     down_piece = column_block(down_proj, down_proj_first, rep_index)
-    in_first_new, in_second_new, in_piece_new = adam_update(
+    in_first_new, in_second_new, in_delta = adam_delta(
         in_piece, in_proj_first, in_proj_second, summed_in / token_count, 0.7 * D ** (-0.5), 0.1
     )
-    out_first_new, out_second_new, out_piece_new = adam_update(
+    out_first_new, out_second_new, out_delta = adam_delta(
         out_piece,
         out_proj_first,
         out_proj_second,
@@ -350,10 +426,10 @@
         0.7 * NOUT ** (-0.5),
         0.1,
     )
-    gu_first_new, gu_second_new, gu_piece_new = adam_update(
+    gu_first_new, gu_second_new, gu_delta = adam_delta(
         gu_piece, gate_up_first, gate_up_second, summed_gu / token_count, 0.7 * D ** (-0.5), 0.1
     )
-    down_first_new, down_second_new, down_piece_new = adam_update(
+    down_first_new, down_second_new, down_delta = adam_delta(
         down_piece,
         down_proj_first,
         down_proj_second,
@@ -361,12 +437,10 @@
         0.7 * FF ** (-0.5),
         0.1,
     )
-    in_new, out_new, gu_new, down_new = (
-        lax.all_gather(in_piece_new, "rep", axis=1, tiled=True),
-        lax.all_gather(out_piece_new, "rep", axis=1, tiled=True),
-        lax.all_gather(gu_piece_new, "rep", axis=1, tiled=True),
-        lax.all_gather(down_piece_new, "rep", axis=1, tiled=True),
-    )
+    down_new = gathered_weight(down_proj, down_delta)
+    gu_new = gathered_weight(gate_up, gu_delta)
+    out_new = gathered_weight(out_proj, out_delta)
+    in_new = gathered_weight(in_proj, in_delta)
     dt_first_new, dt_second_new, dt_new = adam_update(
         dt_proj, dt_proj_first, dt_proj_second, summed_dt / token_count, 0.7 * D ** (-0.5), 0.1
     )
@@ -467,4 +541,5 @@
         P(),
         P(),
     )
-    return jax.shard_map(local, mesh=mesh, in_specs=in_specs, out_specs=out_specs, check_vma=False)
+    step = functools.partial(local, mesh.shape["rep"], mesh.shape["shard"])
+    return jax.shard_map(step, mesh=mesh, in_specs=in_specs, out_specs=out_specs, check_vma=False)

time: 1230 us -> 812 us (0.66)
  waiting for transfers between devices: 894 us -> 511 us
  blocking collectives: 111 us -> 51.6 us
  local copies, waits for them, and re-layouts: 47.2 us -> 77.6 us
    reduce_scatter x9 -> x6, waiting for transfers between devices: 555 us -> 160 us  [the longest x4 111 us: summed_block(): lax.psum_scatter(grad.astype(jnp.bfloat16), 'shard', scatter_dimension=0,...]
    all_gather x8, waiting for transfers between devices: 338 us -> 201 us  [the longest x4 110 us: gather_weight(): mine = lax.all_gather(mine, 'shard', axis=0, tiled=True)]
    psum x0 -> x1, waiting for transfers between devices: none -> 121 us  [local(): lax.psum(jnp.concatenate([grad_dt.reshape(-1), grad_gains, d_conv.reshape...]
    psum x1 -> x0, blocking collectives: 29.4 us -> none  [local(): lax.psum((owned_dt, owned_gains, owned_conv), 'rep')]
    unnamed x19, waiting for transfers between devices: 0.3 us -> 27.5 us
    add x1 -> x4, other arithmetic: 0.2 us -> 17.6 us  [gathered_weight(): weight + lax.all_gather(delta, 'rep', axis=1, tiled=True).astype(jnp.floa...]
    all_gather x3 -> x1, blocking collectives: 26.1 us -> 9.75 us  [local(): small = lax.all_gather(small, 'shard', axis=0)]
    unnamed x1 -> x0, blocking collectives: 16 us -> none
  transfers between devices with their start and end apart: 18 -> 29, of which waited for: 16 -> 17; matrix products, arithmetic and copies ran while one was open for 13% -> 26% of each run, Pallas kernels for 0% -> 0%
where the time goes in v1:
time: 812 us; the launch traced here: 806 us
  waiting for transfers between devices  511 us (63%)
  matrix products  80.5 us (10%)
  local copies, waits for them, and re-layouts  77.6 us (10%)
  other arithmetic  65.2 us (8%)
  blocking collectives  51.6 us (6%)
  between operations  16.9 us (2%)
    psum x1, waiting for transfers between devices, local(): lax.psum(jnp.concatenate([grad_dt.reshape(-1), grad_gains, d_conv.reshape...  121 us
    reduce_scatter x4, waiting for transfers between devices, summed_block(): lax.psum_scatter(grad.astype(jnp.bfloat16), 'shard', scatter_dimension=0,...  111 us
    all_gather x4, waiting for transfers between devices, gather_weight(): mine = lax.all_gather(mine, 'shard', axis=0, tiled=True)  110 us
    all_gather x4, waiting for transfers between devices, gathered_weight(): lax.all_gather(delta, 'rep', axis=1, tiled=True).astype(jnp.float32)  90.8 us
    reduce_scatter x2, waiting for transfers between devices, summed_block(): lax.psum_scatter(owned, 'rep', scatter_dimension=1, axis_index_groups=gro...  49 us
    psum x1, blocking collectives, local(): token_count = lax.psum(token_local, ('rep', 'shard'))  41.9 us
    unnamed x266, local copies, waits for them, and re-layouts  30.2 us
    dot_general x9, matrix products, right_product(): lax.dot_general(left, right, (((1,), (1,)), ((), ())), preferred_element_...  28.9 us
  transfers between devices with their start and end apart: 29, of which 17 were waited for; matrix products, arithmetic and copies ran while one was open for 26% of the time, Pallas kernels for 0%

profile of v1, /device:TPU:0, one launch (start us, length us, event | category | flops | bytes accessed | tf_op | source)
XLA Modules:
  0.0 806.5 jit_solution(12599719688800899875)
XLA Ops:
  22.3 41.9 %psum.14 = f32[]{:T(128)} all-reduce(f32[]{:T(128)S(6)} %convert_element_type.157), channel_id=1, replica_groups=mesh['rep'=8,'shard'=4] {'rep','shard'}, use_global_device_ids=true, to_apply=%region_1.0 | all-reduce | flops 1 | bytes 8 | tf_op jit(solution)/shard_map/psum | solution.py:252
  64.6 9.7 %all-gather = bf16[4,1,9280]{2,1,0:T(2,128)(2,1)S(1)} all-gather(bf16[1,1,9280]{2,1,0:T(2,128)(2,1)S(1)} %maximum_bitcast_fusion), channel_id=1, replica_groups=mesh['rep'=8,'shard'=4] {'shard'}, dimensions={0}, use_global_device_ids=true | all-gather | bytes 92800 | tf_op jit(solution)/shard_map/all_gather | solution.py:256
  84.6 20.7 %all-gather.12.cloned.1.call-done = bf16[2048,512]{1,0:T(8,128)(2,1)} async-done(((bf16[512,512]{1,0:T(8,128)(2,1)}), bf16[2048,512]{1,0:T(8,128)(2,1)}) %all-gather.12.cloned.1.call-update) | async-done | bytes 2097168 | tf_op jit(solution)/shard_map/all_gather | solution.py:162
  105.3 37.8 %all-gather.16.cloned.1.call-done = bf16[2048,512]{1,0:T(8,128)(2,1)} async-done(((bf16[512,512]{1,0:T(8,128)(2,1)}), bf16[2048,512]{1,0:T(8,128)(2,1)}) %all-gather.16.cloned.1.call-update) | async-done | bytes 2097168 | tf_op jit(solution)/shard_map/all_gather | solution.py:162
  143.0 3.4 fusion.111
  146.4 51.6 %all-gather.14.cloned.1.call-done = bf16[1024,2048]{1,0:T(8,128)(2,1)} async-done(((bf16[256,2048]{1,0:T(8,128)(2,1)}), bf16[1024,2048]{1,0:T(8,128)(2,1)}) %all-gather.14.cloned.1.call-update) | async-done | bytes 4194320 | tf_op jit(solution)/shard_map/all_gather | solution.py:162
  212.6 4.6 fusion.15
  231.1 3.9 fusion.154
  236.7 4.6 multiply_reduce_fusion.10
  253.3 3.4 fusion.108
  267.0 4.0 multiply_reduce_fusion.6
  276.7 5.9 fusion.42
  288.2 3.4 convolution_convert_fusion.2
  313.0 5.5 constant_dynamic-slice_fusion.3
  323.6 4.4 convolution_convert_fusion
  342.7 54.1 %reduce-scatter.19.cloned.1.call-done = bf16[256,2048]{1,0:T(8,128)(2,1)} async-done(((bf16[1024,2048]{1,0:T(8,128)(2,1)}), bf16[256,2048]{1,0:T(8,128)(2,1)}) %reduce-scatter.19.cloned.1.call-update) | async-done | bytes 1048592 | tf_op jit(solution)/shard_map/reduce_scatter | solution.py:193
  398.0 55.3 %reduce-scatter.13.cloned.1.call-done = bf16[256,2048]{1,0:T(8,128)(2,1)} async-done(((bf16[1024,2048]{1,0:T(8,128)(2,1)}), bf16[256,2048]{1,0:T(8,128)(2,1)}) %reduce-scatter.13.cloned.1.call-update) | async-done | bytes 1048592 | tf_op jit(solution)/shard_map/reduce_scatter | solution.py:193
  455.1 3.8 fusion.88
  459.0 5.3 fusion.70
  469.6 8.2 %reduce-scatter.25.cloned.1.call-done = bf16[128,512]{1,0:T(8,128)(2,1)} async-done(((bf16[512,512]{1,0:T(8,128)(2,1)}), bf16[128,512]{1,0:T(8,128)(2,1)}) %reduce-scatter.25.cloned.1.call-update) | async-done | bytes 131088
  481.5 18.9 %reduce-scatter.27.cloned.1.call-done = bf16[128,512]{1,0:T(8,128)(2,1)} async-done(((bf16[512,512]{1,0:T(8,128)(2,1)}), bf16[128,512]{1,0:T(8,128)(2,1)}) %reduce-scatter.27.cloned.1.call-update) | async-done | bytes 131088
  504.2 24.0 %reduce-scatter.21.cloned.1.call-done = bf16[256,512]{1,0:T(8,128)(2,1)} async-done(((bf16[256,2048]{1,0:T(8,128)(2,1)}), bf16[256,512]{1,0:T(8,128)(2,1)}) %reduce-scatter.21.cloned.1.call-update) | async-done | bytes 262160 | tf_op jit(solution)/shard_map/reduce_scatter | solution.py:197
  531.4 24.9 %reduce-scatter.15.cloned.1.call-done = bf16[256,512]{1,0:T(8,128)(2,1)} async-done(((bf16[256,2048]{1,0:T(8,128)(2,1)}), bf16[256,512]{1,0:T(8,128)(2,1)}) %reduce-scatter.15.cloned.1.call-update) | async-done | bytes 262160 | tf_op jit(solution)/shard_map/reduce_scatter | solution.py:197
  556.3 3.4 fusion.75
  561.5 120.7 %all-reduce.26.cloned.1.call-done = f32[37192]{0:T(1024)} async-done(((f32[37192]{0:T(1024)}), f32[37192]{0:T(1024)}) %all-reduce.26.cloned.1.call-update) | async-done | bytes 148784 | tf_op jit(solution)/shard_map/psum | solution.py:393
  691.2 18.4 %all-gather.20.cloned.1.call-done = bf16[512,1024]{1,0:T(8,128)(2,1)} async-done(((bf16[512,128]{1,0:T(8,128)(2,1)}), bf16[512,1024]{1,0:T(8,128)(2,1)}) %all-gather.20.cloned.1.call-update) | async-done | bytes 1048592 | tf_op jit(solution)/shard_map/all_gather | solution.py:209
  712.5 21.2 %all-gather.24.cloned.1.call-done = bf16[512,1024]{1,0:T(8,128)(2,1)} async-done(((bf16[512,128]{1,0:T(8,128)(2,1)}), bf16[512,1024]{1,0:T(8,128)(2,1)}) %all-gather.24.cloned.1.call-update) | async-done | bytes 1048592 | tf_op jit(solution)/shard_map/all_gather | solution.py:209
  733.7 3.6 convert_add_fusion.2
  737.3 26.2 %all-gather.22.cloned.1.call-done = bf16[256,4096]{1,0:T(8,128)(2,1)} async-done(((bf16[256,512]{1,0:T(8,128)(2,1)}), bf16[256,4096]{1,0:T(8,128)(2,1)}) %all-gather.22.cloned.1.call-update) | async-done | bytes 2097168 | tf_op jit(solution)/shard_map/all_gather | solution.py:209
  763.5 5.6 convert_add_fusion
  769.1 25.1 %all-gather.18.cloned.1.call-done = bf16[256,4096]{1,0:T(8,128)(2,1)} async-done(((bf16[256,512]{1,0:T(8,128)(2,1)}), bf16[256,4096]{1,0:T(8,128)(2,1)}) %all-gather.18.cloned.1.call-update) | async-done | bytes 2097168 | tf_op jit(solution)/shard_map/all_gather | solution.py:209
  794.1 5.6 convert_add_fusion.1
  (499 shorter events, 160.4 us)
Async XLA Ops:
  7.2 67.3 %all-gather.10.cloned.1.call-start = ((), (), s32[]{:S(2)}) async-start(), calls=%async_computation.8 | async-start | bytes 5242880 | tf_op jit(solution)/shard_map/all_gather | solution.py:162
  10.0 95.3 %all-gather.12.cloned.1.call-start = ((), (), s32[]{:S(2)}) async-start(), calls=%async_computation.9 | async-start | bytes 2621440 | tf_op jit(solution)/shard_map/all_gather | solution.py:162
  12.2 130.9 %all-gather.16.cloned.1.call-start = ((), (), s32[]{:S(2)}) async-start(), calls=%async_computation.11 | async-start | bytes 2621440 | tf_op jit(solution)/shard_map/all_gather | solution.py:162
  14.3 183.7 %all-gather.14.cloned.1.call-start = ((), (), s32[]{:S(2)}) async-start(), calls=%async_computation.10 | async-start | bytes 5242880 | tf_op jit(solution)/shard_map/all_gather | solution.py:162
  17.2 319.8 %reduce-scatter.17.cloned.1.call-start = ((), (), s32[]{:S(2)}) async-start(), calls=%async_computation.16 | async-start | bytes 2621440 | tf_op jit(solution)/shard_map/reduce_scatter | solution.py:193
  21.8 265.8 %collective-permute-start.11 = (bf16[128,512]{0,1:T(8,128)(2,1)}, bf16[128,512]{0,1:T(8,128)(2,1)}, u32[]{:S(2)}, u32[]{:S(2)}) collective-permute-start(bf16[128,512]{0,1:T(8,128)(2,1)} %bitcast.60), channel_id=1, source_target_pairs={{0,4},{4,0},{8,12},{12,8},{16,20},{20,16},{24,28},{28,24},{1,5},{5... | collective-permute-start | bytes 393224 | tf_op jit(solution)/shard_map/ppermute | solution.py:157
  74.5 126.5 %collective-permute-start = (bf16[1024,2048]{1,0:T(8,128)(2,1)}, bf16[1024,2048]{1,0:T(8,128)(2,1)}, u32[]{:S(2)}, u32[]{:S(2)}) collective-permute-start(bf16[1024,2048]{1,0:T(8,128)(2,1)} %all-gather.10.cloned.1.call-done), channel_id=1, source_target_pairs={{0,4},{4,0},{8,12},{12,8},{16,20},{20,16},{24,28},{28,24},{1,5},{5... | collective-permute-start | bytes 12582920 | tf_op jit(solution)/shard_map/ppermute | solution.py:157
  81.0 131.5 %copy-start.86 = (pred[128,128]{1,0:T(8,128)(4,1)}, pred[128,128]{1,0:T(8,128)(4,1)S(1)}, u32[]{:S(2)}) copy-start(pred[128,128]{1,0:T(8,128)(4,1)S(1)} %copy.203) | copy-start | bytes 49156
  105.3 118.6 %collective-permute-start.1 = (bf16[2048,512]{1,0:T(8,128)(2,1)}, bf16[2048,512]{1,0:T(8,128)(2,1)}, u32[]{:S(2)}, u32[]{:S(2)}) collective-permute-start(bf16[2048,512]{1,0:T(8,128)(2,1)} %all-gather.12.cloned.1.call-done), channel_id=1, source_target_pairs={{0,4},{4,0},{8,12},{12,8},{16,20},{20,16},{24,28},{28,24},{1,5},{5... | collective-permute-start | bytes 6291464 | tf_op jit(solution)/shard_map/ppermute | solution.py:157
  143.0 88.0 %collective-permute-start.3 = (bf16[2048,512]{1,0:T(8,128)(2,1)}, bf16[2048,512]{1,0:T(8,128)(2,1)}, u32[]{:S(2)}, u32[]{:S(2)}) collective-permute-start(bf16[2048,512]{1,0:T(8,128)(2,1)} %all-gather.16.cloned.1.call-done), channel_id=1, source_target_pairs={{0,4},{4,0},{8,12},{12,8},{16,20},{20,16},{24,28},{28,24},{1,5},{5... | collective-permute-start | bytes 6291464 | tf_op jit(solution)/shard_map/ppermute | solution.py:157
  198.0 30.0 %collective-permute-start.2 = (bf16[1024,2048]{1,0:T(8,128)(2,1)}, bf16[1024,2048]{1,0:T(8,128)(2,1)}, u32[]{:S(2)}, u32[]{:S(2)}) collective-permute-start(bf16[1024,2048]{1,0:T(8,128)(2,1)} %all-gather.14.cloned.1.call-done), channel_id=1, source_target_pairs={{0,4},{4,0},{8,12},{12,8},{16,20},{20,16},{24,28},{28,24},{1,5},{5... | collective-permute-start | bytes 12582920 | tf_op jit(solution)/shard_map/ppermute | solution.py:157
  241.3 46.3 %collective-permute-start.10 = (bf16[128,2048]{1,0:T(8,128)(2,1)}, bf16[128,2048]{1,0:T(8,128)(2,1)}, u32[]{:S(2)}, u32[]{:S(2)}) collective-permute-start(bf16[128,2048]{1,0:T(8,128)(2,1)} %get-tuple-element.170), channel_id=1, source_target_pairs={{0,4},{4,0},{8,12},{12,8},{16,20},{20,16},{24,28},{28,24},{1,5},{5... | collective-permute-start | bytes 1572872 | tf_op jit(solution)/shard_map/ppermute | solution.py:157
  252.8 10.3 %collective-permute-start.7 = (bf16[128,512]{0,1:T(8,128)(2,1)}, bf16[128,512]{0,1:T(8,128)(2,1)}, u32[]{:S(2)}, u32[]{:S(2)}) collective-permute-start(bf16[128,512]{0,1:T(8,128)(2,1)} %bitcast.193), channel_id=1, source_target_pairs={{0,4},{4,0},{8,12},{12,8},{16,20},{20,16},{24,28},{28,24},{1,5},{5... | collective-permute-start | bytes 393224 | tf_op jit(solution)/shard_map/ppermute | solution.py:157
  252.8 10.3 %collective-permute-start.6 = (bf16[128,2048]{1,0:T(8,128)(2,1)}, bf16[128,2048]{1,0:T(8,128)(2,1)}, u32[]{:S(2)}, u32[]{:S(2)}) collective-permute-start(bf16[128,2048]{1,0:T(8,128)(2,1)} %pad_maximum_fusion.2), channel_id=1, source_target_pairs={{0,4},{4,0},{8,12},{12,8},{16,20},{20,16},{24,28},{28,24},{1,5},{5... | collective-permute-start | bytes 1572872 | tf_op jit(solution)/shard_map/ppermute | solution.py:157
  266.3 74.3 %reduce-scatter.23.cloned.1.call-start = ((), (), s32[]{:S(2)}) async-start(), calls=%async_computation.21 | async-start | bytes 2621440 | tf_op jit(solution)/shard_map/reduce_scatter | solution.py:193
  291.7 105.1 %reduce-scatter.19.cloned.1.call-start = ((), (), s32[]{:S(2)}) async-start(), calls=%async_computation.18 | async-start | bytes 5242880 | tf_op jit(solution)/shard_map/reduce_scatter | solution.py:193
  321.1 2.6 collective-permute-start.9
  321.2 2.5 collective-permute-start.8
  328.0 125.3 %reduce-scatter.13.cloned.1.call-start = ((), (), s32[]{:S(2)}) async-start(), calls=%async_computation.12 | async-start | bytes 5242880 | tf_op jit(solution)/shard_map/reduce_scatter | solution.py:193
  331.1 2.3 collective-permute-start.5
  331.3 2.1 collective-permute-start.4
  336.9 140.9 %reduce-scatter.25.cloned.1.call-start = ((), (), s32[]{:S(2)}) async-start(), calls=%async_computation.23 | async-start | bytes 655360
  339.1 161.3 %reduce-scatter.27.cloned.1.call-start = ((), (), s32[]{:S(2)}) async-start(), calls=%async_computation.24 | async-start | bytes 655360
  342.6 185.6 %reduce-scatter.21.cloned.1.call-start = ((), (), s32[]{:S(2)}) async-start(), calls=%async_computation.19 | async-start | bytes 1310720 | tf_op jit(solution)/shard_map/reduce_scatter | solution.py:197
  396.8 159.5 %reduce-scatter.15.cloned.1.call-start = ((), (), s32[]{:S(2)}) async-start(), calls=%async_computation.13 | async-start | bytes 1310720 | tf_op jit(solution)/shard_map/reduce_scatter | solution.py:197
  453.4 228.8 %all-reduce.26.cloned.1.call-start = ((), (), s32[]{:S(2)}) async-start(), calls=%async_computation.15 | async-start | bytes 303104 | tf_op jit(solution)/shard_map/psum | solution.py:393
  469.5 240.1 %all-gather.20.cloned.1.call-start = ((), (), s32[]{:S(2)}) async-start(), calls=%async_computation.17 | async-start | bytes 1179648 | tf_op jit(solution)/shard_map/all_gather | solution.py:209
  481.5 252.2 %all-gather.24.cloned.1.call-start = ((), (), s32[]{:S(2)}) async-start(), calls=%async_computation.22 | async-start | bytes 1179648 | tf_op jit(solution)/shard_map/all_gather | solution.py:209
  504.2 259.3 %all-gather.22.cloned.1.call-start = ((), (), s32[]{:S(2)}) async-start(), calls=%async_computation.20 | async-start | bytes 2359296 | tf_op jit(solution)/shard_map/all_gather | solution.py:209
  531.3 262.8 %all-gather.18.cloned.1.call-start = ((), (), s32[]{:S(2)}) async-start(), calls=%async_computation.14 | async-start | bytes 2359296 | tf_op jit(solution)/shard_map/all_gather | solution.py:209
  559.8 130.8 %copy-start.59 = (f32[256,24]{0,1:T(8,128)S(1)}, f32[256,24]{0,1:T(8,128)}, u32[]{:S(2)}) copy-start(f32[256,24]{0,1:T(8,128)} %param.33) | copy-start | bytes 73732
  559.8 130.8 %copy-start.82 = (f32[256,24]{0,1:T(8,128)S(1)}, f32[256,24]{0,1:T(8,128)}, u32[]{:S(2)}) copy-start(f32[256,24]{0,1:T(8,128)} %param.35) | copy-start | bytes 73732
  (122 other events, 4128.3 us)
Sparse Core Ops, SparseCore 0:
  10.5 56.7 all-gather.9
  69.7 35.5 all-gather.11
  107.7 35.2 all-gather.15
  145.3 52.6 all-gather.13
  266.4 35.1 reduce-scatter.16
  305.3 35.1 reduce-scatter.22
  344.1 52.6 reduce-scatter.18
  400.6 52.6 reduce-scatter.12
  456.2 21.5 reduce-scatter.24
  480.5 19.8 reduce-scatter.26
  502.7 25.4 reduce-scatter.20
  530.5 25.7 reduce-scatter.14
  562.4 119.7 all-reduce.25
  683.6 25.9 all-gather.19
  711.1 22.5 all-gather.23
  735.7 27.6 all-gather.21
  765.5 28.5 all-gather.17
